TPU v7x, 1024 devices: a whole 4x8x16 slice. The times are simulated.
1024 devices in a mesh: dp: 8 (over x, core), expert: 64 (over z, y_lo), etp: 2 (over y_hi).
Axes of the slice: x: 4, y: 8 (y_hi: 2, y_lo: 4; y = y_hi * 4 + y_lo), z: 16, core: 2. Of those that a mesh axis runs over, the one named last changes fastest.
Arguments:
- tokens: bfloat16 [12288, 2048], P(('dp', 'expert')), may hold values from -6 to 6
- cotangent: bfloat16 [12288, 2048], P(('dp', 'expert')), may hold values from -6 to 6
- scores: float32 [8, 32, 96], P('dp'), may hold values from 0.1 to 1
- chosen: int32 [8, 32, 96], P('dp'), may hold values from 0 to 1535, as said below
- w_gate: bfloat16 [64, 2048, 3584], P('expert', None, ('dp', 'etp')), may hold values from -0.125 to 0.125
- w_up: bfloat16 [64, 2048, 3584], P('expert', None, ('dp', 'etp')), may hold values from -0.125 to 0.125
- w_down: bfloat16 [64, 3584, 2048], P('expert', ('dp', 'etp')), may hold values from -0.0625 to 0.0625
Outputs:
- grad_tokens: bfloat16 [12288, 2048], P(('dp', 'expert'), 'etp')
Inputs may be any that keep to these rules, and one draw needn't show every extreme that they name: chosen[r, e] names 96 different tokens of replica r, ordered by holder (token // 24), in any order within one holder; one expert takes at most 2 tokens of one holder, in every replica some expert takes exactly 2 of some holder, and the experts take 2 * 24 entries from every holder in all.
All inputs are finite; a program needn't handle non-finite values.
Results may differ from a plain program's by a relative error of at most 0.023.
Values may be sent and summed in bfloat16 or wider, within the bound.
A program may use at most 64 MiB of HBM per device.

v0:
```python
import jax
import jax.numpy as jnp
from jax import lax
from jax.sharding import PartitionSpec as P


def compact_rows(collect, received):
    return jnp.einsum("csj,sjd->cd", collect, received, preferred_element_type=jnp.float32).astype(
        jnp.bfloat16
    )


def body(tokens, cotangent, scores, chosen, w_gate, w_up, w_down):
    local_rows, model_width = tokens.shape
    experts = chosen.shape[1]
    capacity = chosen.shape[2]
    holders = lax.axis_size("expert")
    replicas = lax.axis_size("dp")
    most_slots = 2 * ((local_rows + experts - 1) // experts)
    holder_index = lax.axis_index("expert")
    expert_id = holder_index // 2
    half_width = model_width // 2
    pick_table = chosen[0]
    holder_of = pick_table // local_rows
    positions = jnp.arange(capacity, dtype=jnp.int32)
    slot_range = jnp.arange(most_slots, dtype=jnp.int32)
    first_slot = jnp.sum((holder_of < holder_index).astype(jnp.int32), axis=1, keepdims=True)
    slot_index = positions[None, :] - first_slot
    is_mine = holder_of == holder_index
    pick_slot = (
        is_mine[:, :, None] & (slot_index[:, :, None] == slot_range[None, None, :])
    ).astype(jnp.bfloat16)
    local_index = pick_table - holder_index * local_rows
    pick_token = (
        local_index[:, :, None] == jnp.arange(local_rows, dtype=jnp.int32)[None, None, :]
    ).astype(jnp.bfloat16)
    sender = jnp.einsum(
        "ecj,eck->ejk", pick_slot, pick_token, preferred_element_type=jnp.float32
    ).astype(jnp.bfloat16)
    own_list = lax.dynamic_index_in_dim(pick_table, expert_id, 0, keepdims=False)
    own_holder = own_list // local_rows
    ahead_count = jnp.sum((own_holder[None, :] < own_holder[:, None]).astype(jnp.int32), axis=1)
    own_slot = positions - ahead_count
    holder_range = jnp.arange(holders, dtype=jnp.int32)
    collect = (
        (own_holder[:, None, None] == holder_range[None, :, None])
        & (own_slot[:, None, None] == slot_range[None, None, :])
    ).astype(jnp.bfloat16)
    gain_row = lax.dynamic_index_in_dim(scores[0], expert_id, 0, keepdims=True)
    gate_local = w_gate[0]
    up_local = w_up[0]
    down_local = w_down[0]
    hidden_local = gate_local.shape[1]

    def pack_whole(values):
        sent_rows = jnp.einsum(
            "ejk,kd->ejd", sender, values, preferred_element_type=jnp.float32
        ).astype(jnp.bfloat16)
        return jnp.repeat(sent_rows, 2, axis=0)

    got_tokens, got_grads = (
        lax.all_to_all(pack_whole(tokens), "expert", split_axis=0, concat_axis=0, tiled=True),
        lax.all_to_all(pack_whole(cotangent), "expert", split_axis=0, concat_axis=0, tiled=True),
    )
    own_tokens = compact_rows(collect, got_tokens)
    own_grads = compact_rows(collect, got_grads)
    all_tokens, all_grads, all_gains = (
        lax.all_gather(own_tokens[None], "dp", axis=0, tiled=True),
        lax.all_gather(own_grads[None], "dp", axis=0, tiled=True),
        lax.all_gather(gain_row.astype(jnp.bfloat16), "dp", axis=0, tiled=True).astype(
            gain_row.dtype
        ),
    )
    gate_value = jnp.einsum(
        "rcd,df->rcf", all_tokens, gate_local, preferred_element_type=jnp.float32
    )
    up_value = jnp.einsum("rcd,df->rcf", all_tokens, up_local, preferred_element_type=jnp.float32)
    back_hidden = jnp.einsum(
        "rcd,fd->rcf", all_grads, down_local, preferred_element_type=jnp.float32
    )
    back_hidden = back_hidden * all_gains[:, :, None]
    sigmoid_gate = jax.nn.sigmoid(gate_value)
    up_grad = (back_hidden * gate_value * sigmoid_gate).astype(jnp.bfloat16)
    gate_grad = (
        back_hidden * up_value * sigmoid_gate * (1.0 + gate_value * (1.0 - sigmoid_gate))
    ).astype(jnp.bfloat16)
    gate_halves = gate_local.reshape(2, half_width, hidden_local)
    up_halves = up_local.reshape(2, half_width, hidden_local)
    partial_rows = jnp.einsum(
        "rcf,hdf->rhcd", gate_grad, gate_halves, preferred_element_type=jnp.float32
    )
    partial_rows = partial_rows + jnp.einsum(
        "rcf,hdf->rhcd", up_grad, up_halves, preferred_element_type=jnp.float32
    )
    own_result = lax.psum_scatter(
        partial_rows.reshape(replicas * 2 * capacity, half_width).astype(jnp.bfloat16),
        ("dp", "etp"),
        scatter_dimension=0,
        tiled=True,
    ).astype(jnp.float32)
    returned = jnp.einsum(
        "csj,cd->sjd", collect.astype(jnp.float32), own_result, precision=lax.Precision.HIGHEST
    )
    arrived = lax.all_to_all(
        returned.astype(jnp.bfloat16), "expert", split_axis=0, concat_axis=0, tiled=True
    ).astype(returned.dtype)
    spread = jnp.repeat(sender.astype(jnp.float32), 2, axis=0)
    grad_tokens = jnp.einsum("ijk,ijd->kd", spread, arrived, precision=lax.Precision.HIGHEST)
    return grad_tokens.astype(jnp.bfloat16)


def solution(mesh):
    placed = (
        P(("dp", "expert"), None),
        P(("dp", "expert"), None),
        P("dp", None, None),
        P("dp", None, None),
        P("expert", None, ("dp", "etp")),
        P("expert", None, ("dp", "etp")),
        P("expert", ("dp", "etp"), None),
    )
    return jax.shard_map(
        body, mesh=mesh, in_specs=placed, out_specs=P(("dp", "expert"), "etp"), check_vma=False
    )
```

profile of v0, /device:TPU:6, one launch (start us, length us, event | category | flops | bytes accessed | tf_op | source)
XLA Modules:
  0.0 322.3 jit_solution(12927802321916516947)
XLA Ops:
  6.5 0.0 copy-start
  6.5 0.0 copy-start.5
  6.5 0.9 convert_reduce_fusion.1
  7.5 0.7 broadcast_compare_fusion
  8.2 0.1 iota_subtract_fusion
  8.3 0.7 subtract_bitcast_fusion
  9.0 0.2 fusion.24
  9.2 0.1 copy.43
  9.3 1.1 convolution_convert_fusion
  10.5 0.3 copy.47
  10.7 1.1 broadcast_in_dim.13
  11.8 0.0 copy-start.2
  11.8 22.9 %all-to-all-start.1 = ((bf16[64,2,2048]{2,1,0:T(2,128)(2,1)}), bf16[64,2,2048]{2,1,0:T(2,128)(2,1)S(1)}, u32[]{:S(2)}, u32[]{:S(2)}) async-start(bf16[64,2,2048]{2,1,0:T(2,128)(2,1)} %bitcast.14), calls=%async_computation.1 | async-start | bytes 1048576 | tf_op jit(solution)/shard_map/all_to_all | solution.py:62
  34.8 0.0 all-gather.8.cloned.1.call-start
  34.9 0.7 bitcast_select_fusion
  35.6 0.2 convert_reduce_fusion
  35.8 0.0 copy-start.3
  35.8 31.8 %all-to-all-done.1 = bf16[64,2,2048]{2,1,0:T(2,128)(2,1)S(1)} async-done(((bf16[64,2,2048]{2,1,0:T(2,128)(2,1)}), bf16[64,2,2048]{2,1,0:T(2,128)(2,1)S(1)}, u32[]{:S(2)}, u32[]{:S(2)}) %all-to-all-start.1) | async-done | bytes 524320 | tf_op jit(solution)/shard_map/all_to_all | solution.py:62
  67.6 1.1 fusion.1
  68.7 0.0 copy-start.1
  68.7 0.0 all-gather.8.cloned.1.call-update
  68.7 0.0 all-gather.6.cloned.1.call-start
  68.8 0.0 copy-done.5
  68.8 0.2 convolution_convert_fusion.1
  69.0 0.3 copy.45
  69.3 0.3 broadcast_in_dim.11
  69.6 37.6 %all_to_all.15 = bf16[64,2,2048]{2,1,0:T(2,128)(2,1)S(1)} all-to-all(bf16[64,2,2048]{2,1,0:T(2,128)(2,1)S(1)} %bitcast.93), channel_id=1, replica_groups=mesh['dp'=8,'expert'=64,'etp'=2] {'expert'}, dimensions={0} | all-to-all | bytes 1048576 | tf_op jit(solution)/shard_map/all_to_all | solution.py:63
  107.2 1.1 fusion
  108.3 0.0 all-gather.6.cloned.1.call-update
  108.3 0.0 reduce-scatter.2.cloned.1.call-start
  108.4 0.7 dynamic-slice_convert_fusion
  109.1 7.5 %all-gather.1 = bf16[8,1,96]{2,1,0:T(2,128)(2,1)S(1)} all-gather(bf16[1,1,96]{2,1,0:T(2,128)(2,1)S(1)} %dynamic-slice_convert_fusion), channel_id=3, replica_groups=mesh['dp'=8,'expert'=64,'etp'=2] {'dp'}, dimensions={0}, use_global_device_ids=true | all-gather | bytes 1728 | tf_op jit(solution)/shard_map/all_gather | solution.py:70
  116.6 0.6 convert_element_type.86
  117.2 0.0 copy-done.2
  117.2 1.6 reshape_squeeze.6
  118.8 0.0 copy-done.3
  118.8 0.0 copy-done.1
  118.8 0.7 reshape_squeeze.7
  119.5 0.0 all-gather.8.cloned.1.call-done
  119.5 3.3 %fusion.10 = f32[8,96,224]{2,1,0:T(8,128)S(1)} fusion(bf16[8,96,2048]{2,1,0:T(8,128)(2,1)} %bitcast.91, bf16[1,2048,224]{1,2,0:T(8,128)(2,1)} %param.11), kind=kOutput, calls=%fused_computation.19 | convolution fusion | flops 704643072 | bytes 4751360 | tf_op jit(solution)/shard_map/rcd,df->rcf/dot_general | solution.py:74
  122.9 15.8 %all-gather.6.cloned.1.call-done = bf16[768,2048]{1,0:T(8,128)(2,1)} async-done(((bf16[96,2048]{1,0:T(8,128)(2,1)}), bf16[768,2048]{1,0:T(8,128)(2,1)}) %all-gather.6.cloned.1.call-update) | async-done | bytes 3145744 | tf_op jit(solution)/shard_map/all_gather | solution.py:69
  138.7 0.0 copy-done
  138.7 3.8 %convolution_multiply_fusion.1 = f32[8,96,224]{2,1,0:T(8,128)} fusion(bf16[8,96,2048]{2,1,0:T(8,128)(2,1)} %bitcast.96, bf16[1,224,2048]{2,1,0:T(8,128)(2,1)S(1)} %copy-done, f32[8,96]{1,0:T(8,128)} %bitcast.95), kind=kOutput, calls=%fused_computation.10 | convolution fusion | flops 704815104 | bytes 4754432 | tf_op jit(solution)/shard_map/rcd,fd->rcf/dot_general | solution.py:78
  142.5 8.4 %fusion.6 = f32[8,96,2,1024]{3,1,2,0:T(8,128)} fusion(f32[8,96,224]{2,1,0:T(8,128)} %convolution_multiply_fusion.1, bf16[8,96,2048]{2,1,0:T(8,128)(2,1)} %bitcast.92, bf16[1,2048,224]{1,2,0:T(8,128)(2,1)S(1)} %copy-done.1, bf16[2,1024,224]{1,0,2:T(2,128)(2,1)} %reshape_squeeze.6, f32[8,96,224]{2,1,0:T(8,128)S(1)} %fusion.10), kind=kOutput, calls=%fused_computation.13 | convolution fusion | flops 1411006464 | bytes 12648448 | tf_op jit(solution)/shard_map/rcf,hdf->rhcd/dot_general | solution.py:89
  151.0 5.9 %add_convert_fusion = bf16[8,96,2,1024]{3,1,2,0:T(8,128)(2,1)} fusion(f32[8,96,2,1024]{3,1,2,0:T(8,128)} %fusion.6, bf16[2,1024,224]{1,0,2:T(2,128)(2,1)S(1)} %reshape_squeeze.7, f32[8,96,224]{2,1,0:T(8,128)} %convolution_multiply_fusion.1, f32[8,96,224]{2,1,0:T(8,128)S(1)} %fusion.10), kind=kOutput, calls=%fused_computation | convolution fusion | flops 708820992 | bytes 11730944 | tf_op jit(solution)/shard_map/rcf,hdf->rhcd/dot_general | solution.py:92
  156.8 0.0 copy-start.4
  156.8 0.0 reduce-scatter.2.cloned.1.call-update
  156.9 119.0 %reduce-scatter.2.cloned.1.call-done = bf16[96,1024]{1,0:T(8,128)(2,1)} async-done(((bf16[1536,1024]{1,0:T(8,128)(2,1)}), bf16[96,1024]{1,0:T(8,128)(2,1)}) %reduce-scatter.2.cloned.1.call-update) | async-done | bytes 196624 | tf_op jit(solution)/shard_map/reduce_scatter | solution.py:95
  275.9 0.0 copy-done.4
  275.9 1.1 convolution_convert_fusion.2
  277.0 1.0 copy.51
  278.0 15.8 %all-to-all-start.2 = ((bf16[64,2,1024]{2,1,0:T(2,128)(2,1)}), bf16[64,2,1024]{2,1,0:T(2,128)(2,1)S(1)}, u32[]{:S(2)}, u32[]{:S(2)}) async-start(bf16[64,2,1024]{2,1,0:T(2,128)(2,1)} %copy.51), calls=%async_computation.3 | async-start | bytes 524288 | tf_op jit(solution)/shard_map/all_to_all | solution.py:104
  293.8 0.1 copy.44
  293.9 21.0 %all-to-all-done.2 = bf16[64,2,1024]{2,1,0:T(2,128)(2,1)S(1)} async-done(((bf16[64,2,1024]{2,1,0:T(2,128)(2,1)}), bf16[64,2,1024]{2,1,0:T(2,128)(2,1)S(1)}, u32[]{:S(2)}, u32[]{:S(2)}) %all-to-all-start.2) | async-done | bytes 262176 | tf_op jit(solution)/shard_map/all_to_all | solution.py:104
  314.9 0.9 fusion.7
  (4 shorter events, 0.0 us)
Async XLA Ops:
  6.5 132.2 %copy-start = (bf16[1,224,2048]{2,1,0:T(8,128)(2,1)S(1)}, bf16[1,224,2048]{2,1,0:T(8,128)(2,1)}, u32[]{:S(2)}) copy-start(bf16[1,224,2048]{2,1,0:T(8,128)(2,1)} %param.13) | copy-start | bytes 2752516
  6.5 62.2 %copy-start.5 = (bf16[24,2048]{1,0:T(8,128)(2,1)S(1)}, bf16[24,2048]{1,0:T(8,128)(2,1)}, u32[]{:S(2)}) copy-start(bf16[24,2048]{1,0:T(8,128)(2,1)} %param.8) | copy-start | bytes 294916
  11.8 105.4 %copy-start.2 = (bf16[1,2048,224]{1,2,0:T(8,128)(2,1)S(1)}, bf16[1,2048,224]{1,2,0:T(8,128)(2,1)}, u32[]{:S(2)}) copy-start(bf16[1,2048,224]{1,2,0:T(8,128)(2,1)} %param.11) | copy-start | bytes 2752516
  11.8 55.8 %all-to-all-start.1 = ((bf16[64,2,2048]{2,1,0:T(2,128)(2,1)}), bf16[64,2,2048]{2,1,0:T(2,128)(2,1)S(1)}, u32[]{:S(2)}, u32[]{:S(2)}) async-start(bf16[64,2,2048]{2,1,0:T(2,128)(2,1)} %bitcast.14), calls=%async_computation.1 | async-start | bytes 1048576 | tf_op jit(solution)/shard_map/all_to_all | solution.py:62
  34.8 84.7 %all-gather.8.cloned.1.call-start = ((), (), s32[]{:S(2)}) async-start(), calls=%async_computation.6 | async-start | bytes 3538944 | tf_op jit(solution)/shard_map/all_gather | solution.py:68
  35.8 83.0 %copy-start.3 = (pred[96,64]{0,1:T(8,128)(4,1)}, pred[96,64]{0,1:T(8,128)(4,1)S(1)}, u32[]{:S(2)}) copy-start(pred[96,64]{0,1:T(8,128)(4,1)S(1)} %iota_compare_fusion.2) | copy-start | bytes 18436
  68.7 50.1 %copy-start.1 = (bf16[1,2048,224]{1,2,0:T(8,128)(2,1)S(1)}, bf16[1,2048,224]{1,2,0:T(8,128)(2,1)}, u32[]{:S(2)}) copy-start(bf16[1,2048,224]{1,2,0:T(8,128)(2,1)} %param.12) | copy-start | bytes 2752516
  68.7 70.0 %all-gather.6.cloned.1.call-start = ((), (), s32[]{:S(2)}) async-start(), calls=%async_computation.5 | async-start | bytes 3538944 | tf_op jit(solution)/shard_map/all_gather | solution.py:69
  108.3 167.5 %reduce-scatter.2.cloned.1.call-start = ((), (), s32[]{:S(2)}) async-start(), calls=%async_computation.4 | async-start | bytes 3342336 | tf_op jit(solution)/shard_map/reduce_scatter | solution.py:95
  156.8 119.0 %copy-start.4 = (pred[96,64]{0,1:T(8,128)(4,1)S(1)}, pred[96,64]{0,1:T(8,128)(4,1)}, u32[]{:S(2)}) copy-start(pred[96,64]{0,1:T(8,128)(4,1)} %copy-done.3) | copy-start | bytes 18436
  278.0 36.9 %all-to-all-start.2 = ((bf16[64,2,1024]{2,1,0:T(2,128)(2,1)}), bf16[64,2,1024]{2,1,0:T(2,128)(2,1)S(1)}, u32[]{:S(2)}, u32[]{:S(2)}) async-start(bf16[64,2,1024]{2,1,0:T(2,128)(2,1)} %copy.51), calls=%async_computation.3 | async-start | bytes 524288 | tf_op jit(solution)/shard_map/all_to_all | solution.py:104
Sparse Core Ops, SparseCore 0:
  68.8 28.3 all-gather.7
  108.5 30.2 all-gather.5
  157.0 118.8 reduce-scatter.1
where the time goes:
time: 323 us; the launch traced here: 322 us
  waiting for transfers between devices  188 us (58%)
  blocking collectives  45.1 us (14%)
  starting transfers between devices  38.9 us (12%)
  matrix products  27.3 us (8%)
  between operations  13.3 us (4%)
  local copies, waits for them, and re-layouts  6.13 us (2%)
  other arithmetic  3.95 us (1%)
    reduce_scatter x1, waiting for transfers between devices, body(): lax.psum_scatter(partial_rows.reshape(replicas * 2 * capacity, half_width...  119 us
    all_to_all x1, blocking collectives, body(): lax.all_to_all(pack_whole(cotangent), 'expert', split_axis=0, concat_axis...  37.6 us
    all_to_all x1, waiting for transfers between devices, body(): lax.all_to_all(pack_whole(tokens), 'expert', split_axis=0, concat_axis=0,...  31.8 us
    all_to_all x1, starting transfers between devices, body(): lax.all_to_all(pack_whole(tokens), 'expert', split_axis=0, concat_axis=0,...  22.9 us
    all_to_all x1, waiting for transfers between devices, body(): lax.all_to_all(returned.astype(jnp.bfloat16), 'expert', split_axis=0, con...  21 us
    all_gather x1, waiting for transfers between devices, body(): lax.all_gather(own_grads[None], 'dp', axis=0, tiled=True)  15.8 us
    all_to_all x1, starting transfers between devices, body(): lax.all_to_all(returned.astype(jnp.bfloat16), 'expert', split_axis=0, con...  15.8 us
    dot_general x1, matrix products, body(): jnp.einsum('rcf,hdf->rhcd', gate_grad, gate_halves, preferred_element_typ...  8.45 us
  transfers between devices with their start and end apart: 5, of which 4 were waited for; matrix products, arithmetic and copies ran while one was open for 3% of the time, Pallas kernels for 0%

commit v1 on v0

v1 whole, which is shorter than its diff:
```python
import functools

import jax
import jax.numpy as jnp
from jax import lax
from jax.experimental import pallas as pl
from jax.experimental.pallas import tpu as pltpu
from jax.sharding import PartitionSpec as P

MESH = pl.DeviceIdType.MESH
SEM = pltpu.SemaphoreType.DMA
FLAT = (((1,), (1,)), ((), ()))


def layer_kernel(
    n_dp,
    packed,
    collect,
    collect_t,
    gain,
    gate_in,
    up_in,
    down_in,
    arrived,
    got,
    rows,
    w_gate,
    w_up,
    w_down,
    gate_up,
    hidden,
    part,
    total,
    direct_out,
    direct_in,
    relay_out,
    relay_in,
    sum_out,
    sum_in,
    pair_out,
    pair_in,
    half_out,
    half_in,
    returned,
    z_send,
    z_recv,
    z_own,
    w_own,
    w_send,
    w_recv,
    y_send,
    y_recv,
    x_send,
    x_recv,
    f_send,
    f_recv,
    d_send,
    d_recv,
    r_send,
    r_recv,
    s_send,
    s_recv,
    p_sem,
    h_sem,
    b_sem,
):
    holders = arrived.shape[0]
    count = rows.shape[3]
    half = rows.shape[4]
    quarter = half // 2
    bf16, f32 = jnp.bfloat16, jnp.float32
    dp = lax.axis_index("dp")
    me = lax.axis_index("expert")
    etp = lax.axis_index("etp")
    q = lax.rem(me, 2)
    core = {"dp": dp + 1 - 2 * lax.rem(dp, 2)}
    right = {"dp": lax.rem(dp + 2, n_dp)}
    left = {"dp": lax.rem(dp + n_dp - 2, n_dp)}
    pair = {"expert": me + 1 - 2 * q}
    other = {"etp": 1 - etp}
    weights = ((gate_in, w_gate), (up_in, w_up), (down_in, w_down))

    def remote(src, dst, send_sem, recv_sem, where):
        return pltpu.make_async_remote_copy(
            src_ref=src,
            dst_ref=dst,
            send_sem=send_sem,
            recv_sem=recv_sem,
            device_id=where,
            device_id_type=MESH,
        )

    barrier = pltpu.get_barrier_semaphore()

    def greet(k, carry):
        peer = {"expert": lax.rem(me + k, holders)}
        pl.semaphore_signal(barrier, inc=1, device_id=peer, device_id_type=MESH)
        return carry

    lax.fori_loop(1, holders, greet, 0)
    for peer in (core, right, left, other):
        pl.semaphore_signal(barrier, inc=1, device_id=peer, device_id_type=MESH)
    own_got = [
        pltpu.make_async_copy(packed.at[kind, me], got.at[kind, me], z_own.at[kind])
        for kind in range(2)
    ]
    own_weights = [
        pltpu.make_async_copy(src.at[0], dst.at[0], w_own.at[i])
        for i, (src, dst) in enumerate(weights)
    ]
    for copy in own_got + own_weights:
        copy.start()
    pl.semaphore_wait(barrier, holders + 3)

    def to_all(send):
        def both_ways(k, carry):
            send(lax.rem(me + k, holders))
            send(lax.rem(me + holders - k, holders))
            return carry

        lax.fori_loop(1, holders // 2, both_ways, 0)
        send(lax.rem(me + holders // 2, holders))

    def dispatch(kind):
        def send(peer):
            remote(
                packed.at[kind, peer],
                got.at[kind, me],
                z_send.at[kind],
                z_recv.at[kind],
                {"expert": peer},
            ).start()

        to_all(send)

    rest = pl.ds(0, holders - 1)

    def all_of(ref, sem):
        pltpu.make_async_copy(ref.at[rest], ref.at[rest], sem).wait()

    dispatch(0)
    given_weights = [
        remote(src.at[0], dst.at[1], w_send.at[i], w_recv.at[i], core)
        for i, (src, dst) in enumerate(weights)
    ]
    for copy in given_weights:
        copy.start()
    dispatch(1)

    def spread(kind, side):
        src = rows.at[kind, 0, side]
        return (
            remote(
                src,
                rows.at[kind, 1, side],
                x_send.at[kind, side, 0],
                x_recv.at[kind, side, 0],
                right,
            ),
            remote(
                src,
                rows.at[kind, 2, side],
                x_send.at[kind, side, 1],
                x_recv.at[kind, side, 1],
                left,
            ),
        )

    def forward(kind, side):
        upper, lower = pl.ds(0, count // 2), pl.ds(count // 2, count // 2)
        return (
            remote(
                rows.at[kind, 1, side, upper],
                rows.at[kind, 3, side, upper],
                f_send.at[kind, side, 0],
                f_recv.at[kind, side, 0],
                right,
            ),
            remote(
                rows.at[kind, 2, side, lower],
                rows.at[kind, 3, side, lower],
                f_send.at[kind, side, 1],
                f_recv.at[kind, side, 1],
                left,
            ),
        )

    swaps, spreads, forwards = [], {}, {}
    for kind in range(2):
        swaps.append(
            remote(
                rows.at[kind, 0, q], rows.at[kind, 0, q], y_send.at[kind], y_recv.at[kind], pair
            )
        )
        for which, side in ((0, q), (1, 1 - q)):
            spreads[kind, which] = spread(kind, side)
            forwards[kind, which] = forward(kind, side)

    def compact(kind):
        own_got[kind].wait()
        all_of(got.at[kind], z_recv.at[kind])
        slots = got[kind].reshape(2 * holders, half)
        rows[kind, 0, q] = jnp.dot(collect[...], slots, preferred_element_type=f32).astype(bf16)
        swaps[kind].start()
        for copy in spreads[kind, 0]:
            copy.start()

    def pass_on(kind, which):
        for arrive, copy in zip(spreads[kind, which], forwards[kind, which]):
            arrive.wait_recv()
            copy.start()

    def times(kind, b, n, weight):
        a = rows[kind, pl.ds(b, n), 0].reshape(n * count, half)
        c = rows[kind, pl.ds(b, n), 1].reshape(n * count, half)
        return lax.dot_general(
            a, weight[:, :half], FLAT, preferred_element_type=f32
        ) + lax.dot_general(c, weight[:, half:], FLAT, preferred_element_type=f32)

    def first_products(b, n):
        def one(w, carry):
            gate_up[0, w, pl.ds(b * count, n * count)] = times(0, b, n, w_gate[w])
            gate_up[1, w, pl.ds(b * count, n * count)] = times(0, b, n, w_up[w])
            return carry

        lax.fori_loop(0, 2, one, 0)

    def hidden_grads(b, n):
        def one(w, carry):
            back = times(1, b, n, w_down[w])
            gate = gate_up[0, w, pl.ds(b * count, n * count)]
            up = gate_up[1, w, pl.ds(b * count, n * count)]
            s = jax.nn.sigmoid(gate)
            here = pl.ds(0, n * count)
            hidden[w, 0, here] = (back * up * s * (1.0 + gate * (1.0 - s))).astype(bf16)
            hidden[w, 1, here] = (back * gate * s).astype(bf16)
            return carry

        lax.fori_loop(0, 2, one, 0)

    def row_grads(b, n, piece):
        at = pl.ds(pl.multiple_of(piece * quarter, quarter), quarter)
        here = pl.ds(0, n * count)
        grad = jnp.zeros((n * count, quarter), f32)
        for w in range(2):
            for i, weight in enumerate((w_gate, w_up)):
                grad += jnp.dot(hidden[w, i, here], weight[w, :, at], preferred_element_type=f32)
        part[pl.ds(b, n), piece] = grad.reshape(n, count, quarter)

    def all_row_grads(b, n):
        def one(piece, carry):
            row_grads(b, n, piece)
            return carry

        lax.fori_loop(0, 4, one, 0)

    compact(0)
    swaps[0].wait_recv()
    for copy in spreads[0, 1]:
        copy.start()
    pass_on(0, 0)
    for copy in own_weights + given_weights:
        copy.wait()
    first_products(0, 1)
    compact(1)
    pass_on(0, 1)
    first_products(1, 2)
    swaps[1].wait_recv()
    for copy in spreads[1, 1]:
        copy.start()
    pass_on(1, 0)
    for copy in forwards[0, 0] + forwards[0, 1]:
        copy.wait_recv()
    first_products(3, 1)
    hidden_grads(0, 1)
    all_row_grads(0, 1)
    pass_on(1, 1)

    hidden_grads(1, 2)
    all_row_grads(1, 2)
    for piece in range(2):
        direct_out[0, piece] = part[2, 2 + piece].astype(bf16)
        direct_out[1, piece] = part[1, piece].astype(bf16)
    direct = [
        remote(direct_out.at[i], direct_in.at[i], d_send.at[i], d_recv.at[i], where)
        for i, where in ((0, right), (1, left))
    ]
    for copy in direct:
        copy.start()
    for copy in forwards[1, 0] + forwards[1, 1]:
        copy.wait_recv()
    hidden_grads(3, 1)

    relays, sums = [], []
    for stage, sub in ((0, 1 - q), (1, q)):
        for i, piece, where in ((0, sub, right), (1, 2 + sub, left)):
            row_grads(3, 1, piece)
            relay_out[i, stage] = part[3, piece].astype(bf16)
            relays.append(
                remote(
                    relay_out.at[i, stage],
                    relay_in.at[i, stage],
                    r_send.at[i, stage],
                    r_recv.at[i, stage],
                    where,
                )
            )
            relays[-1].start()
    for stage, sub in ((0, 1 - q), (1, q)):
        for i, b, piece, where in ((0, 2, sub, right), (1, 1, 2 + sub, left)):
            relays[2 * stage + i].wait_recv()
            sum_out[i, stage] = (part[b, piece] + relay_in[i, stage].astype(f32)).astype(bf16)
            sums.append(
                remote(
                    sum_out.at[i, stage],
                    sum_in.at[i, stage],
                    s_send.at[i, stage],
                    s_recv.at[i, stage],
                    where,
                )
            )
            sums[-1].start()
    for copy in direct:
        copy.wait_recv()
    weight = gain[...]

    def along_x(stage, sub, i):
        sums[2 * stage + i].wait_recv()
        terms = sum_in[i, stage].astype(f32) + direct_in[1 - i, sub].astype(f32)
        return (part[0, 2 * i + sub] + terms) * weight

    for i in range(2):
        pair_out[i] = along_x(0, 1 - q, i).astype(bf16)
    pair_swap = remote(pair_out, pair_in, p_sem.at[0], p_sem.at[1], pair)
    pair_swap.start()
    for i in range(2):
        total[i] = along_x(1, q, i)
    pair_swap.wait_recv()
    half_out[...] = (total[1 - etp] + pair_in[1 - etp].astype(f32)).astype(bf16)
    half_swap = remote(half_out, half_in, h_sem.at[0], h_sem.at[1], other)
    half_swap.start()
    mine = total[etp] + pair_in[etp].astype(f32)
    half_swap.wait_recv()
    result = (mine + half_in[...].astype(f32)).astype(bf16)

    slots = jnp.dot(collect_t[...], result, preferred_element_type=f32).astype(bf16)
    returned[...] = slots.reshape(holders, 2, quarter)
    own_back = pltpu.make_async_copy(returned.at[me], arrived.at[me], b_sem.at[2])
    own_back.start()

    def send_back(peer):
        remote(
            returned.at[peer], arrived.at[me], b_sem.at[0], b_sem.at[1], {"expert": peer}
        ).start()

    to_all(send_back)
    own_back.wait()
    all_of(returned, b_sem.at[0])
    for kind in range(2):
        all_of(packed.at[kind], z_send.at[kind])
    copies = swaps + direct + relays + sums + [pair_swap, half_swap]
    for key in spreads:
        copies += spreads[key] + forwards[key]
    for copy in copies:
        copy.wait_send()
    all_of(arrived, b_sem.at[1])


def layer(n_dp, packed, collect, gain, gate, up, down):
    holders, most_slots, half = packed.shape[1:]
    count = collect.shape[0]
    quarter = half // 2
    slice_width = gate.shape[1]
    bf16, f32 = jnp.bfloat16, jnp.float32
    any_spec = pl.BlockSpec(memory_space=pl.ANY)
    vmem_spec = pl.BlockSpec(memory_space=pltpu.VMEM)
    slices = pltpu.VMEM((2, slice_width, 2 * half), bf16)
    quarters = pltpu.VMEM((2, 2, count, quarter), bf16)
    two_quarters = pltpu.VMEM((2, count, quarter), bf16)
    one_quarter = pltpu.VMEM((count, quarter), bf16)
    return pl.pallas_call(
        functools.partial(layer_kernel, n_dp),
        out_shape=jax.ShapeDtypeStruct((holders, most_slots, quarter), bf16),
        in_specs=[any_spec, vmem_spec, vmem_spec, vmem_spec, any_spec, any_spec, any_spec],
        out_specs=any_spec,
        scratch_shapes=[
            pltpu.VMEM((2, holders, most_slots, half), bf16),
            pltpu.VMEM((2, 4, 2, count, half), bf16),
            slices,
            slices,
            slices,
            pltpu.VMEM((2, 2, 4 * count, slice_width), f32),
            pltpu.VMEM((2, 2, 2 * count, slice_width), bf16),
            pltpu.VMEM((4, 4, count, quarter), f32),
            pltpu.VMEM((2, count, quarter), f32),
            quarters,
            quarters,
            quarters,
            quarters,
            quarters,
            quarters,
            two_quarters,
            two_quarters,
            one_quarter,
            one_quarter,
            pltpu.VMEM((holders, most_slots, quarter), bf16),
            SEM((2,)),
            SEM((2,)),
            SEM((2,)),
            SEM((3,)),
            SEM((3,)),
            SEM((3,)),
            SEM((2,)),
            SEM((2,)),
            SEM((2, 2, 2)),
            SEM((2, 2, 2)),
            SEM((2, 2, 2)),
            SEM((2, 2, 2)),
            SEM((2,)),
            SEM((2,)),
            SEM((2, 2)),
            SEM((2, 2)),
            SEM((2, 2)),
            SEM((2, 2)),
            SEM((2,)),
            SEM((2,)),
            SEM((3,)),
        ],
        compiler_params=pltpu.CompilerParams(
            collective_id=0, has_side_effects=True, vmem_limit_bytes=40 * 1024 * 1024
        ),
    )(packed, collect, collect.T, gain, gate, up, down)


def body(tokens, cotangent, scores, chosen, w_gate, w_up, w_down):
    local_rows, model_width = tokens.shape
    experts = chosen.shape[1]
    capacity = chosen.shape[2]
    holders = lax.axis_size("expert")
    most_slots = 2 * ((local_rows + experts - 1) // experts)
    holder_index = lax.axis_index("expert")
    expert_id = holder_index // 2
    pick_table = chosen[0]
    holder_of = pick_table // local_rows
    positions = jnp.arange(capacity, dtype=jnp.int32)
    slot_range = jnp.arange(most_slots, dtype=jnp.int32)
    first_slot = jnp.sum((holder_of < holder_index).astype(jnp.int32), axis=1, keepdims=True)
    slot_index = positions[None, :] - first_slot
    is_mine = holder_of == holder_index
    pick_slot = (
        is_mine[:, :, None] & (slot_index[:, :, None] == slot_range[None, None, :])
    ).astype(jnp.bfloat16)
    local_index = pick_table - holder_index * local_rows
    pick_token = (
        local_index[:, :, None] == jnp.arange(local_rows, dtype=jnp.int32)[None, None, :]
    ).astype(jnp.bfloat16)
    sender = jnp.einsum(
        "ecj,eck->ejk", pick_slot, pick_token, preferred_element_type=jnp.float32
    ).astype(jnp.bfloat16)
    own_list = lax.dynamic_index_in_dim(pick_table, expert_id, 0, keepdims=False)
    own_holder = own_list // local_rows
    ahead_count = jnp.sum((own_holder[None, :] < own_holder[:, None]).astype(jnp.int32), axis=1)
    own_slot = positions - ahead_count
    holder_range = jnp.arange(holders, dtype=jnp.int32)
    collect = (
        (own_holder[:, None, None] == holder_range[None, :, None])
        & (own_slot[:, None, None] == slot_range[None, None, :])
    ).astype(jnp.bfloat16)
    gain = lax.dynamic_index_in_dim(scores[0], expert_id, 0, keepdims=False)[:, None]

    stacked = jnp.stack([tokens, cotangent]).reshape(2, local_rows, 2, model_width // 2)
    packed = jnp.einsum(
        "ejk,akqd->aeqjd", sender, stacked, preferred_element_type=jnp.float32
    ).astype(jnp.bfloat16)
    arrived = layer(
        lax.axis_size("dp"),
        packed.reshape(2, holders, most_slots, model_width // 2),
        collect.reshape(capacity, holders * most_slots),
        gain,
        jnp.swapaxes(w_gate, 1, 2),
        jnp.swapaxes(w_up, 1, 2),
        w_down,
    ).reshape(experts, 2, most_slots, model_width // 4)
    grad_tokens = jnp.einsum(
        "ejk,eqjd->kqd", sender, arrived, preferred_element_type=jnp.float32
    )
    return grad_tokens.reshape(local_rows, model_width // 2).astype(jnp.bfloat16)


def solution(mesh):
    placed = (
        P(("dp", "expert"), None),
        P(("dp", "expert"), None),
        P("dp", None, None),
        P("dp", None, None),
        P("expert", None, ("dp", "etp")),
        P("expert", None, ("dp", "etp")),
        P("expert", ("dp", "etp"), None),
    )
    return jax.shard_map(
        body, mesh=mesh, in_specs=placed, out_specs=P(("dp", "expert"), "etp"), check_vma=False
    )
```

time: 323 us -> 110 us (0.34)
  waiting for transfers between devices: 188 us -> 0 us
  Pallas kernels: 0 us -> 105 us
  blocking collectives: 45.1 us -> 0 us
  starting transfers between devices: 38.9 us -> 0 us
  matrix products: 27.3 us -> 1.38 us
  between operations: 13.3 us -> 0.21 us
  local copies, waits for them, and re-layouts: 6.13 us -> 2.18 us
  other arithmetic: 3.95 us -> 0.47 us
    reduce_scatter x1 -> x0, waiting for transfers between devices: 119 us -> none  [body(): lax.psum_scatter(partial_rows.reshape(replicas * 2 * capacity, half_width...]
    pallas_call x0 -> x1, Pallas kernels: none -> 105 us  [layer(): pl.pallas_call(functools.partial(layer_kernel, n_dp), out_shape=jax.Shape...]
    all_to_all x2 -> x0, waiting for transfers between devices: 52.8 us -> none  [the longest x1 31.8 us: body(): lax.all_to_all(pack_whole(tokens), 'expert', split_axis=0, concat_axis=0,...]
    all_to_all x2 -> x0, starting transfers between devices: 38.8 us -> none  [the longest x1 22.9 us: body(): lax.all_to_all(pack_whole(tokens), 'expert', split_axis=0, concat_axis=0,...]
    all_to_all x1 -> x0, blocking collectives: 37.6 us -> none  [body(): lax.all_to_all(pack_whole(cotangent), 'expert', split_axis=0, concat_axis...]
    dot_general x10 -> x2, matrix products: 27 us -> 1.16 us  [the longest x1 0.82 us: body(): jnp.einsum('ejk,eqjd->kqd', sender, arrived, preferred_element_type=jnp.f...]
    all_gather x2 -> x0, waiting for transfers between devices: 15.9 us -> none  [the longest x1 15.8 us: body(): lax.all_gather(own_grads[None], 'dp', axis=0, tiled=True)]
    all_gather x1 -> x0, blocking collectives: 7.54 us -> none  [body(): lax.all_gather(gain_row.astype(jnp.bfloat16), 'dp', axis=0, tiled=True)]
  transfers between devices with their start and end apart: 5 -> 0, of which waited for: 4 -> 0; matrix products, arithmetic and copies ran while one was open for 3% -> 0% of each run, Pallas kernels for 0% -> 0%
where the time goes in v1:
time: 110 us
  Pallas kernels  105 us (95%)
  local copies, waits for them, and re-layouts  2.18 us (2%)
  matrix products  1.38 us (1%)
    pallas_call x1, Pallas kernels, layer(): pl.pallas_call(functools.partial(layer_kernel, n_dp), out_shape=jax.Shape...  105 us

profile of v1, /device:TPU:6, one launch (start us, length us, event | category | flops | bytes accessed | tf_op | source)
XLA Modules:
  0.0 109.7 jit_solution(16800157093502388980)
XLA Ops:
  0.0 0.0 copy-start
  0.0 0.0 copy-start.5
  0.0 0.0 copy-start.4
  0.0 1.0 stack.10
  1.0 0.0 copy-start.3
  1.0 0.0 copy-done.5
  1.1 0.0 copy-done.4
  1.2 0.1 convert_reduce_fusion.1
  1.3 0.1 iota_subtract_fusion
  1.4 0.2 fusion.2
  1.6 0.1 copy.30
  1.7 0.0 copy-start.1
  1.7 0.0 copy-start.2
  1.7 0.3 fusion
  2.0 0.5 copy.33
  2.6 0.2 convert_reduce_fusion
  2.9 0.1 copy.34.collect
  3.0 0.0 copy-done
  3.0 0.1 copy.35.gain
  3.1 0.0 copy-done.3
  3.1 0.0 copy-done.1
  3.1 0.1 copy-done.2
  3.2 105.5 %shard_map.73 = bf16[64,2,512]{2,1,0:T(2,128)(2,1)S(1)} custom-call(bf16[2,64,2,1024]{3,2,1,0:T(2,128)(2,1)S(1)} %bitcast.51, bf16[96,128]{1,0:T(8,128)(2,1)S(1)} %copy.34.collect, bf16[128,96]{1,0:T(8,128)(2,1)S(1)} %bitcast.56, f32[96,1]{1,0:T(8,128)S(1)} %copy.35.gain, bf16[1,224,2048]{2,1,0:T(8,128)(2,1)S(1)} %bitcast.52, ...), custom_call_target="tpu_custom_call" | custom-call | tf_op jit(solution)/shard_map/pallas_call | solution.py:381
  108.7 0.1 copy.36
  108.8 0.1 dot_general.16
  108.9 0.8 fusion.1
  (11 shorter events, 0.2 us)
Async XLA Ops:
  0.0 3.0 %copy-start = (f32[1,32,96]{2,1,0:T(8,128)S(1)}, f32[1,32,96]{2,1,0:T(8,128)}, u32[]{:S(2)}) copy-start(f32[1,32,96]{2,1,0:T(8,128)} %param.9) | copy-start | bytes 36868
  0.0 1.0 copy-start.5
  0.0 1.1 %copy-start.4 = (s32[1,32,96]{2,1,0:T(8,128)S(1)}, s32[1,32,96]{2,1,0:T(8,128)}, u32[]{:S(2)}) copy-start(s32[1,32,96]{2,1,0:T(8,128)} %param.10) | copy-start | bytes 36868
  1.0 2.1 %copy-start.3 = (bf16[1,224,2048]{2,1,0:T(8,128)(2,1)S(1)}, bf16[1,224,2048]{2,1,0:T(8,128)(2,1)}, u32[]{:S(2)}) copy-start(bf16[1,224,2048]{2,1,0:T(8,128)(2,1)} %down_in.1) | copy-start | bytes 2752516
  1.7 1.5 %copy-start.1 = (bf16[1,2048,224]{1,2,0:T(8,128)(2,1)S(1)}, bf16[1,2048,224]{1,2,0:T(8,128)(2,1)}, u32[]{:S(2)}) copy-start(bf16[1,2048,224]{1,2,0:T(8,128)(2,1)} %param.11) | copy-start | bytes 2752516
  1.7 1.5 %copy-start.2 = (bf16[1,2048,224]{1,2,0:T(8,128)(2,1)S(1)}, bf16[1,2048,224]{1,2,0:T(8,128)(2,1)}, u32[]{:S(2)}) copy-start(bf16[1,2048,224]{1,2,0:T(8,128)(2,1)} %param.12) | copy-start | bytes 2752516

commit v2 on v1

--- a/solution.py
+++ b/solution.py
@@ -50,6 +50,7 @@
     w_recv,
     y_send,
     y_recv,
+    o_sem,
     x_send,
     x_recv,
     f_send,
@@ -60,14 +61,15 @@
     r_recv,
     s_send,
     s_recv,
-    p_sem,
+    p_send,
+    p_recv,
     h_sem,
     b_sem,
 ):
     holders = arrived.shape[0]
     count = rows.shape[3]
-    half = rows.shape[4]
-    quarter = half // 2
+    quarter = rows.shape[4]
+    upper, lower = pl.ds(0, count // 2), pl.ds(count // 2, count // 2)
     bf16, f32 = jnp.bfloat16, jnp.float32
     dp = lax.axis_index("dp")
     me = lax.axis_index("expert")
@@ -78,6 +80,7 @@
     left = {"dp": lax.rem(dp + n_dp - 2, n_dp)}
     pair = {"expert": me + 1 - 2 * q}
     other = {"etp": 1 - etp}
+    chunks = ((0, etp), (1, etp), (1, 1 - etp), (0, 1 - etp))
     weights = ((gate_in, w_gate), (up_in, w_up), (down_in, w_down))
 
     def remote(src, dst, send_sem, recv_sem, where):
@@ -101,8 +104,8 @@
     for peer in (core, right, left, other):
         pl.semaphore_signal(barrier, inc=1, device_id=peer, device_id_type=MESH)
     own_got = [
-        pltpu.make_async_copy(packed.at[kind, me], got.at[kind, me], z_own.at[kind])
-        for kind in range(2)
+        pltpu.make_async_copy(packed.at[kind, p, me], got.at[c, me], z_own.at[c])
+        for c, (kind, p) in enumerate(chunks[:3])
     ]
     own_weights = [
         pltpu.make_async_copy(src.at[0], dst.at[0], w_own.at[i])
@@ -121,13 +124,15 @@
         lax.fori_loop(1, holders // 2, both_ways, 0)
         send(lax.rem(me + holders // 2, holders))
 
-    def dispatch(kind):
+    def dispatch(c):
+        kind, p = chunks[c]
+
         def send(peer):
             remote(
-                packed.at[kind, peer],
-                got.at[kind, me],
-                z_send.at[kind],
-                z_recv.at[kind],
+                packed.at[kind, p, peer],
+                got.at[c, me],
+                z_send.at[c],
+                z_recv.at[c],
                 {"expert": peer},
             ).start()
 
@@ -147,75 +152,79 @@
         copy.start()
     dispatch(1)
 
-    def spread(kind, side):
-        src = rows.at[kind, 0, side]
-        return (
+    def spread(c, which):
+        kind, p = chunks[c]
+        at = 2 * (q if which == 0 else 1 - q) + p
+        src = rows.at[kind, 0, at]
+        return tuple(
             remote(
                 src,
-                rows.at[kind, 1, side],
-                x_send.at[kind, side, 0],
-                x_recv.at[kind, side, 0],
-                right,
-            ),
+                rows.at[kind, 1 + i, at],
+                x_send.at[c, which, i],
+                x_recv.at[c, which, i],
+                where,
+            )
+            for i, where in ((0, right), (1, left))
+        )
+
+    def forward(c, which):
+        kind, p = chunks[c]
+        at = 2 * (q if which == 0 else 1 - q) + p
+        return tuple(
             remote(
-                src,
-                rows.at[kind, 2, side],
-                x_send.at[kind, side, 1],
-                x_recv.at[kind, side, 1],
-                left,
-            ),
+                rows.at[kind, 1 + i, at, part_of],
+                rows.at[kind, 3, at, part_of],
+                f_send.at[c, which, i],
+                f_recv.at[c, which, i],
+                where,
+            )
+            for i, part_of, where in ((0, upper, right), (1, lower, left))
         )
 
-    def forward(kind, side):
-        upper, lower = pl.ds(0, count // 2), pl.ds(count // 2, count // 2)
-        return (
-            remote(
-                rows.at[kind, 1, side, upper],
-                rows.at[kind, 3, side, upper],
-                f_send.at[kind, side, 0],
-                f_recv.at[kind, side, 0],
-                right,
-            ),
-            remote(
-                rows.at[kind, 2, side, lower],
-                rows.at[kind, 3, side, lower],
-                f_send.at[kind, side, 1],
-                f_recv.at[kind, side, 1],
-                left,
-            ),
-        )
-
     swaps, spreads, forwards = [], {}, {}
-    for kind in range(2):
-        swaps.append(
-            remote(
-                rows.at[kind, 0, q], rows.at[kind, 0, q], y_send.at[kind], y_recv.at[kind], pair
-            )
-        )
-        for which, side in ((0, q), (1, 1 - q)):
-            spreads[kind, which] = spread(kind, side)
-            forwards[kind, which] = forward(kind, side)
-
-    def compact(kind):
-        own_got[kind].wait()
-        all_of(got.at[kind], z_recv.at[kind])
-        slots = got[kind].reshape(2 * holders, half)
-        rows[kind, 0, q] = jnp.dot(collect[...], slots, preferred_element_type=f32).astype(bf16)
-        swaps[kind].start()
-        for copy in spreads[kind, 0]:
+    for c, (kind, p) in enumerate(chunks):
+        mine = rows.at[kind, 0, 2 * q + p]
+        swaps.append(remote(mine, mine, y_send.at[c], y_recv.at[c], pair))
+        for which in range(2):
+            spreads[c, which] = spread(c, which)
+            forwards[c, which] = forward(c, which)
+    crossed = rows.at[0, 0, 2 * q + etp]
+    cross = remote(crossed, crossed, o_sem.at[0], o_sem.at[1], other)
+
+    def send_own(c):
+        swaps[c].start()
+        for copy in spreads[c, 0]:
             copy.start()
 
-    def pass_on(kind, which):
-        for arrive, copy in zip(spreads[kind, which], forwards[kind, which]):
+    def compact(c):
+        kind, p = chunks[c]
+        own_got[c].wait()
+        all_of(got.at[c], z_recv.at[c])
+        slots = got[c].reshape(2 * holders, quarter)
+        dense = jnp.dot(collect[...], slots, preferred_element_type=f32)
+        rows[kind, 0, 2 * q + p] = dense.astype(bf16)
+
+    def send_pairs(c):
+        swaps[c].wait_recv()
+        for copy in spreads[c, 1]:
+            copy.start()
+
+    def pass_on(c, which):
+        for arrive, copy in zip(spreads[c, which], forwards[c, which]):
             arrive.wait_recv()
             copy.start()
 
+    def passed(c):
+        for copy in forwards[c, 0] + forwards[c, 1]:
+            copy.wait_recv()
+
     def times(kind, b, n, weight):
-        a = rows[kind, pl.ds(b, n), 0].reshape(n * count, half)
-        c = rows[kind, pl.ds(b, n), 1].reshape(n * count, half)
-        return lax.dot_general(
-            a, weight[:, :half], FLAT, preferred_element_type=f32
-        ) + lax.dot_general(c, weight[:, half:], FLAT, preferred_element_type=f32)
+        total_of = jnp.zeros((n * count, weight.shape[0]), f32)
+        for piece in range(4):
+            a = rows[kind, pl.ds(b, n), piece].reshape(n * count, quarter)
+            columns = weight[:, piece * quarter : (piece + 1) * quarter]
+            total_of += lax.dot_general(a, columns, FLAT, preferred_element_type=f32)
+        return total_of
 
     def first_products(b, n):
         def one(w, carry):
@@ -255,47 +264,57 @@
         lax.fori_loop(0, 4, one, 0)
 
     compact(0)
-    swaps[0].wait_recv()
-    for copy in spreads[0, 1]:
-        copy.start()
+    cross.start()
+    send_own(0)
+    dispatch(2)
+    send_pairs(0)
     pass_on(0, 0)
+    compact(1)
+    send_own(1)
+    pass_on(0, 1)
+    cross.wait_recv()
+    send_own(3)
+    send_pairs(1)
+    pass_on(1, 0)
+    compact(2)
+    send_own(2)
+    pass_on(1, 1)
+    send_pairs(3)
+    pass_on(3, 0)
+    send_pairs(2)
+    pass_on(2, 0)
     for copy in own_weights + given_weights:
         copy.wait()
     first_products(0, 1)
-    compact(1)
-    pass_on(0, 1)
+    pass_on(3, 1)
     first_products(1, 2)
-    swaps[1].wait_recv()
-    for copy in spreads[1, 1]:
-        copy.start()
-    pass_on(1, 0)
-    for copy in forwards[0, 0] + forwards[0, 1]:
-        copy.wait_recv()
+    hidden_grads(0, 1)
+    pass_on(2, 1)
+    all_row_grads(0, 1)
+    passed(0)
+    passed(3)
     first_products(3, 1)
-    hidden_grads(0, 1)
-    all_row_grads(0, 1)
-    pass_on(1, 1)
 
     hidden_grads(1, 2)
     all_row_grads(1, 2)
-    for piece in range(2):
-        direct_out[0, piece] = part[2, 2 + piece].astype(bf16)
-        direct_out[1, piece] = part[1, piece].astype(bf16)
+    direct_out[0] = part[2, :, lower].astype(bf16)
+    direct_out[1] = part[1, :, upper].astype(bf16)
     direct = [
         remote(direct_out.at[i], direct_in.at[i], d_send.at[i], d_recv.at[i], where)
         for i, where in ((0, right), (1, left))
     ]
     for copy in direct:
         copy.start()
-    for copy in forwards[1, 0] + forwards[1, 1]:
-        copy.wait_recv()
+    passed(1)
+    passed(2)
     hidden_grads(3, 1)
 
+    order = (2 * (1 - etp) + 1 - q, 2 * (1 - etp) + q, 2 * etp + 1 - q, 2 * etp + q)
     relays, sums = [], []
-    for stage, sub in ((0, 1 - q), (1, q)):
-        for i, piece, where in ((0, sub, right), (1, 2 + sub, left)):
-            row_grads(3, 1, piece)
-            relay_out[i, stage] = part[3, piece].astype(bf16)
+    for stage, piece in enumerate(order):
+        row_grads(3, 1, piece)
+        for i, part_of, where in ((0, upper, right), (1, lower, left)):
+            relay_out[i, stage] = part[3, piece, part_of].astype(bf16)
             relays.append(
                 remote(
                     relay_out.at[i, stage],
@@ -306,10 +325,11 @@
                 )
             )
             relays[-1].start()
-    for stage, sub in ((0, 1 - q), (1, q)):
-        for i, b, piece, where in ((0, 2, sub, right), (1, 1, 2 + sub, left)):
+    for stage, piece in enumerate(order):
+        for i, b, part_of, where in ((0, 2, upper, right), (1, 1, lower, left)):
             relays[2 * stage + i].wait_recv()
-            sum_out[i, stage] = (part[b, piece] + relay_in[i, stage].astype(f32)).astype(bf16)
+            added = part[b, piece, part_of] + relay_in[i, stage].astype(f32)
+            sum_out[i, stage] = added.astype(bf16)
             sums.append(
                 remote(
                     sum_out.at[i, stage],
@@ -322,26 +342,33 @@
             sums[-1].start()
     for copy in direct:
         copy.wait_recv()
-    weight = gain[...]
-
-    def along_x(stage, sub, i):
-        sums[2 * stage + i].wait_recv()
-        terms = sum_in[i, stage].astype(f32) + direct_in[1 - i, sub].astype(f32)
-        return (part[0, 2 * i + sub] + terms) * weight
-
-    for i in range(2):
-        pair_out[i] = along_x(0, 1 - q, i).astype(bf16)
-    pair_swap = remote(pair_out, pair_in, p_sem.at[0], p_sem.at[1], pair)
-    pair_swap.start()
-    for i in range(2):
-        total[i] = along_x(1, q, i)
-    pair_swap.wait_recv()
-    half_out[...] = (total[1 - etp] + pair_in[1 - etp].astype(f32)).astype(bf16)
+
+    def along_x(stage):
+        piece = order[stage]
+        pieces = []
+        for i, part_of in ((0, upper), (1, lower)):
+            sums[2 * stage + i].wait_recv()
+            terms = sum_in[i, stage].astype(f32) + direct_in[1 - i, piece].astype(f32)
+            pieces.append((part[0, piece, part_of] + terms) * gain[part_of, :])
+        return jnp.concatenate(pieces, axis=0)
+
+    pair_swaps = [
+        remote(pair_out.at[i], pair_in.at[i], p_send.at[i], p_recv.at[i], pair) for i in range(2)
+    ]
+    pair_out[0] = along_x(0).astype(bf16)
+    pair_swaps[0].start()
+    total[...] = along_x(1)
+    pair_swaps[0].wait_recv()
+    half_out[...] = (total[...] + pair_in[0].astype(f32)).astype(bf16)
     half_swap = remote(half_out, half_in, h_sem.at[0], h_sem.at[1], other)
     half_swap.start()
-    mine = total[etp] + pair_in[etp].astype(f32)
+    pair_out[1] = along_x(2).astype(bf16)
+    pair_swaps[1].start()
+    total[...] = along_x(3)
+    pair_swaps[1].wait_recv()
+    total[...] += pair_in[1].astype(f32)
     half_swap.wait_recv()
-    result = (mine + half_in[...].astype(f32)).astype(bf16)
+    result = (total[...] + half_in[...].astype(f32)).astype(bf16)
 
     slots = jnp.dot(collect_t[...], result, preferred_element_type=f32).astype(bf16)
     returned[...] = slots.reshape(holders, 2, quarter)
@@ -356,9 +383,9 @@
     to_all(send_back)
     own_back.wait()
     all_of(returned, b_sem.at[0])
-    for kind in range(2):
-        all_of(packed.at[kind], z_send.at[kind])
-    copies = swaps + direct + relays + sums + [pair_swap, half_swap]
+    for c, (kind, p) in enumerate(chunks[:3]):
+        all_of(packed.at[kind, p], z_send.at[c])
+    copies = swaps + direct + relays + sums + pair_swaps + [cross, half_swap]
     for key in spreads:
         copies += spreads[key] + forwards[key]
     for copy in copies:
@@ -367,15 +394,14 @@
 
 
 def layer(n_dp, packed, collect, gain, gate, up, down):
-    holders, most_slots, half = packed.shape[1:]
+    holders, most_slots, quarter = packed.shape[2:]
     count = collect.shape[0]
-    quarter = half // 2
     slice_width = gate.shape[1]
     bf16, f32 = jnp.bfloat16, jnp.float32
     any_spec = pl.BlockSpec(memory_space=pl.ANY)
     vmem_spec = pl.BlockSpec(memory_space=pltpu.VMEM)
-    slices = pltpu.VMEM((2, slice_width, 2 * half), bf16)
-    quarters = pltpu.VMEM((2, 2, count, quarter), bf16)
+    slices = pltpu.VMEM((2, slice_width, 4 * quarter), bf16)
+    half_rows = pltpu.VMEM((2, 4, count // 2, quarter), bf16)
     two_quarters = pltpu.VMEM((2, count, quarter), bf16)
     one_quarter = pltpu.VMEM((count, quarter), bf16)
     return pl.pallas_call(
@@ -384,44 +410,46 @@
         in_specs=[any_spec, vmem_spec, vmem_spec, vmem_spec, any_spec, any_spec, any_spec],
         out_specs=any_spec,
         scratch_shapes=[
-            pltpu.VMEM((2, holders, most_slots, half), bf16),
-            pltpu.VMEM((2, 4, 2, count, half), bf16),
+            pltpu.VMEM((3, holders, most_slots, quarter), bf16),
+            pltpu.VMEM((2, 4, 4, count, quarter), bf16),
             slices,
             slices,
             slices,
             pltpu.VMEM((2, 2, 4 * count, slice_width), f32),
             pltpu.VMEM((2, 2, 2 * count, slice_width), bf16),
             pltpu.VMEM((4, 4, count, quarter), f32),
-            pltpu.VMEM((2, count, quarter), f32),
-            quarters,
-            quarters,
-            quarters,
-            quarters,
-            quarters,
-            quarters,
+            pltpu.VMEM((count, quarter), f32),
+            half_rows,
+            half_rows,
+            half_rows,
+            half_rows,
+            half_rows,
+            half_rows,
             two_quarters,
             two_quarters,
             one_quarter,
             one_quarter,
             pltpu.VMEM((holders, most_slots, quarter), bf16),
+            SEM((3,)),
+            SEM((3,)),
+            SEM((3,)),
+            SEM((3,)),
+            SEM((3,)),
+            SEM((3,)),
+            SEM((4,)),
+            SEM((4,)),
+            SEM((2,)),
+            SEM((4, 2, 2)),
+            SEM((4, 2, 2)),
+            SEM((4, 2, 2)),
+            SEM((4, 2, 2)),
             SEM((2,)),
             SEM((2,)),
+            SEM((2, 4)),
+            SEM((2, 4)),
+            SEM((2, 4)),
+            SEM((2, 4)),
             SEM((2,)),
-            SEM((3,)),
-            SEM((3,)),
-            SEM((3,)),
-            SEM((2,)),
-            SEM((2,)),
-            SEM((2, 2, 2)),
-            SEM((2, 2, 2)),
-            SEM((2, 2, 2)),
-            SEM((2, 2, 2)),
-            SEM((2,)),
-            SEM((2,)),
-            SEM((2, 2)),
-            SEM((2, 2)),
-            SEM((2, 2)),
-            SEM((2, 2)),
             SEM((2,)),
             SEM((2,)),
             SEM((3,)),
@@ -468,13 +496,13 @@
     ).astype(jnp.bfloat16)
     gain = lax.dynamic_index_in_dim(scores[0], expert_id, 0, keepdims=False)[:, None]
 
-    stacked = jnp.stack([tokens, cotangent]).reshape(2, local_rows, 2, model_width // 2)
+    stacked = jnp.stack([tokens, cotangent]).reshape(2, local_rows, 2, 2, model_width // 4)
     packed = jnp.einsum(
-        "ejk,akqd->aeqjd", sender, stacked, preferred_element_type=jnp.float32
+        "ejk,akqpd->apeqjd", sender, stacked, preferred_element_type=jnp.float32
     ).astype(jnp.bfloat16)
     arrived = layer(
         lax.axis_size("dp"),
-        packed.reshape(2, holders, most_slots, model_width // 2),
+        packed.reshape(2, 2, holders, most_slots, model_width // 4),
         collect.reshape(capacity, holders * most_slots),
         gain,
         jnp.swapaxes(w_gate, 1, 2),

time: 110 us -> 111 us (level)
  no operation moved by 1% of the time
where the time goes in v2:
time: 111 us; the launch traced here: 110 us
  Pallas kernels  106 us (95%)
  local copies, waits for them, and re-layouts  2.18 us (2%)
  matrix products  1.38 us (1%)
    pallas_call x1, Pallas kernels, layer(): pl.pallas_call(functools.partial(layer_kernel, n_dp), out_shape=jax.Shape...  106 us

profile of v2, /device:TPU:6, one launch (start us, length us, event | category | flops | bytes accessed | tf_op | source)
XLA Modules:
  0.0 110.3 jit_solution(4986096238158530588)
XLA Ops:
  0.0 0.0 copy-start
  0.0 0.0 copy-start.5
  0.0 0.0 copy-start.4
  0.0 1.0 stack.10
  1.0 0.0 copy-start.3
  1.0 0.0 copy-done.5
  1.1 0.0 copy-done.4
  1.2 0.1 convert_reduce_fusion.1
  1.3 0.1 iota_subtract_fusion
  1.4 0.2 fusion.2
  1.6 0.1 copy.30
  1.7 0.0 copy-start.1
  1.7 0.0 copy-start.2
  1.7 0.3 fusion
  2.0 0.5 copy.33
  2.6 0.2 convert_reduce_fusion
  2.9 0.1 copy.34.collect
  3.0 0.0 copy-done
  3.0 0.1 copy.35.gain
  3.1 0.0 copy-done.3
  3.1 0.0 copy-done.1
  3.1 0.1 copy-done.2
  3.2 106.0 %shard_map.73 = bf16[64,2,512]{2,1,0:T(2,128)(2,1)S(1)} custom-call(bf16[2,2,64,2,512]{4,3,2,1,0:T(2,128)(2,1)S(1)} %bitcast.51, bf16[96,128]{1,0:T(8,128)(2,1)S(1)} %copy.34.collect, bf16[128,96]{1,0:T(8,128)(2,1)S(1)} %bitcast.56, f32[96,1]{1,0:T(8,128)S(1)} %copy.35.gain, bf16[1,224,2048]{2,1,0:T(8,128)(2,1)S(1)} %bitcast.52, ...), custom_call_target="tpu_custom_call" | custom-call | tf_op jit(solution)/shard_map/pallas_call | solution.py:407
  109.3 0.1 copy.36
  109.4 0.1 dot_general.16
  109.5 0.8 fusion.1
  (11 shorter events, 0.2 us)
Async XLA Ops:
  0.0 3.0 %copy-start = (f32[1,32,96]{2,1,0:T(8,128)S(1)}, f32[1,32,96]{2,1,0:T(8,128)}, u32[]{:S(2)}) copy-start(f32[1,32,96]{2,1,0:T(8,128)} %param.9) | copy-start | bytes 36868
  0.0 1.0 copy-start.5
  0.0 1.1 %copy-start.4 = (s32[1,32,96]{2,1,0:T(8,128)S(1)}, s32[1,32,96]{2,1,0:T(8,128)}, u32[]{:S(2)}) copy-start(s32[1,32,96]{2,1,0:T(8,128)} %param.10) | copy-start | bytes 36868
  1.0 2.1 %copy-start.3 = (bf16[1,224,2048]{2,1,0:T(8,128)(2,1)S(1)}, bf16[1,224,2048]{2,1,0:T(8,128)(2,1)}, u32[]{:S(2)}) copy-start(bf16[1,224,2048]{2,1,0:T(8,128)(2,1)} %down_in.1) | copy-start | bytes 2752516
  1.7 1.5 %copy-start.1 = (bf16[1,2048,224]{1,2,0:T(8,128)(2,1)S(1)}, bf16[1,2048,224]{1,2,0:T(8,128)(2,1)}, u32[]{:S(2)}) copy-start(bf16[1,2048,224]{1,2,0:T(8,128)(2,1)} %param.11) | copy-start | bytes 2752516
  1.7 1.5 %copy-start.2 = (bf16[1,2048,224]{1,2,0:T(8,128)(2,1)S(1)}, bf16[1,2048,224]{1,2,0:T(8,128)(2,1)}, u32[]{:S(2)}) copy-start(bf16[1,2048,224]{1,2,0:T(8,128)(2,1)} %param.12) | copy-start | bytes 2752516

commit v3 on v2

--- a/solution.py
+++ b/solution.py
@@ -51,6 +51,8 @@
     y_send,
     y_recv,
     o_sem,
+    l_send,
+    l_recv,
     x_send,
     x_recv,
     f_send,
@@ -185,9 +187,16 @@
     for c, (kind, p) in enumerate(chunks):
         mine = rows.at[kind, 0, 2 * q + p]
         swaps.append(remote(mine, mine, y_send.at[c], y_recv.at[c], pair))
-        for which in range(2):
+        for which in range(1 if c < 2 else 2):
             spreads[c, which] = spread(c, which)
             forwards[c, which] = forward(c, which)
+
+    def hand_over(c, source):
+        kind, p = chunks[c]
+        block = rows.at[kind, source, 2 * q + p]
+        return remote(block, block, l_send.at[c, source - 1], l_recv.at[c, source - 1], pair)
+
+    handed = {(c, source): hand_over(c, source) for c in range(2) for source in (1, 2, 3)}
     crossed = rows.at[0, 0, 2 * q + etp]
     cross = remote(crossed, crossed, o_sem.at[0], o_sem.at[1], other)
 
@@ -213,6 +222,17 @@
         for arrive, copy in zip(spreads[c, which], forwards[c, which]):
             arrive.wait_recv()
             copy.start()
+
+    def pass_and_hand(c):
+        for i in range(2):
+            spreads[c, 0][i].wait_recv()
+            forwards[c, 0][i].start()
+            handed[c, 1 + i].start()
+
+    def hand_opposite(c):
+        for copy in forwards[c, 0]:
+            copy.wait_recv()
+        handed[c, 3].start()
 
     def passed(c):
         for copy in forwards[c, 0] + forwards[c, 1]:
@@ -267,34 +287,38 @@
     cross.start()
     send_own(0)
     dispatch(2)
-    send_pairs(0)
-    pass_on(0, 0)
+    pass_and_hand(0)
     compact(1)
     send_own(1)
-    pass_on(0, 1)
     cross.wait_recv()
     send_own(3)
-    send_pairs(1)
-    pass_on(1, 0)
+    hand_opposite(0)
+    pass_and_hand(1)
+    send_pairs(3)
     compact(2)
     send_own(2)
-    pass_on(1, 1)
-    send_pairs(3)
     pass_on(3, 0)
+    hand_opposite(1)
     send_pairs(2)
     pass_on(2, 0)
     for copy in own_weights + given_weights:
         copy.wait()
+    swaps[0].wait_recv()
     first_products(0, 1)
     pass_on(3, 1)
+    handed[0, 1].wait_recv()
+    handed[0, 2].wait_recv()
     first_products(1, 2)
+    swaps[1].wait_recv()
     hidden_grads(0, 1)
     pass_on(2, 1)
     all_row_grads(0, 1)
-    passed(0)
+    handed[0, 3].wait_recv()
     passed(3)
     first_products(3, 1)
 
+    handed[1, 1].wait_recv()
+    handed[1, 2].wait_recv()
     hidden_grads(1, 2)
     all_row_grads(1, 2)
     direct_out[0] = part[2, :, lower].astype(bf16)
@@ -305,7 +329,7 @@
     ]
     for copy in direct:
         copy.start()
-    passed(1)
+    handed[1, 3].wait_recv()
     passed(2)
     hidden_grads(3, 1)
 
@@ -386,6 +410,7 @@
     for c, (kind, p) in enumerate(chunks[:3]):
         all_of(packed.at[kind, p], z_send.at[c])
     copies = swaps + direct + relays + sums + pair_swaps + [cross, half_swap]
+    copies += list(handed.values())
     for key in spreads:
         copies += spreads[key] + forwards[key]
     for copy in copies:
@@ -439,6 +464,8 @@
             SEM((4,)),
             SEM((4,)),
             SEM((2,)),
+            SEM((2, 3)),
+            SEM((2, 3)),
             SEM((4, 2, 2)),
             SEM((4, 2, 2)),
             SEM((4, 2, 2)),

time: 111 us -> 112 us (level)
  no operation moved by 1% of the time
where the time goes in v3:
time: 112 us; the launch traced here: 111 us
  Pallas kernels  107 us (96%)
  local copies, waits for them, and re-layouts  2.18 us (2%)
  matrix products  1.38 us (1%)
    pallas_call x1, Pallas kernels, layer(): pl.pallas_call(functools.partial(layer_kernel, n_dp), out_shape=jax.Shape...  107 us

profile of v3, /device:TPU:6, one launch (start us, length us, event | category | flops | bytes accessed | tf_op | source)
XLA Modules:
  0.0 110.8 jit_solution(707075010960295229)
XLA Ops:
  0.0 0.0 copy-start
  0.0 0.0 copy-start.5
  0.0 0.0 copy-start.4
  0.0 1.0 stack.10
  1.0 0.0 copy-start.3
  1.0 0.0 copy-done.5
  1.1 0.0 copy-done.4
  1.2 0.1 convert_reduce_fusion.1
  1.3 0.1 iota_subtract_fusion
  1.4 0.2 fusion.2
  1.6 0.1 copy.30
  1.7 0.0 copy-start.1
  1.7 0.0 copy-start.2
  1.7 0.3 fusion
  2.0 0.5 copy.33
  2.6 0.2 convert_reduce_fusion
  2.9 0.1 copy.34.collect
  3.0 0.0 copy-done
  3.0 0.1 copy.35.gain
  3.1 0.0 copy-done.3
  3.1 0.0 copy-done.1
  3.1 0.1 copy-done.2
  3.2 106.5 %shard_map.73 = bf16[64,2,512]{2,1,0:T(2,128)(2,1)S(1)} custom-call(bf16[2,2,64,2,512]{4,3,2,1,0:T(2,128)(2,1)S(1)} %bitcast.51, bf16[96,128]{1,0:T(8,128)(2,1)S(1)} %copy.34.collect, bf16[128,96]{1,0:T(8,128)(2,1)S(1)} %bitcast.56, f32[96,1]{1,0:T(8,128)S(1)} %copy.35.gain, bf16[1,224,2048]{2,1,0:T(8,128)(2,1)S(1)} %bitcast.52, ...), custom_call_target="tpu_custom_call" | custom-call | tf_op jit(solution)/shard_map/pallas_call | solution.py:432
  109.8 0.1 copy.36
  109.9 0.1 dot_general.16
  110.0 0.8 fusion.1
  (11 shorter events, 0.2 us)
Async XLA Ops:
  0.0 3.0 %copy-start = (f32[1,32,96]{2,1,0:T(8,128)S(1)}, f32[1,32,96]{2,1,0:T(8,128)}, u32[]{:S(2)}) copy-start(f32[1,32,96]{2,1,0:T(8,128)} %param.9) | copy-start | bytes 36868
  0.0 1.0 copy-start.5
  0.0 1.1 %copy-start.4 = (s32[1,32,96]{2,1,0:T(8,128)S(1)}, s32[1,32,96]{2,1,0:T(8,128)}, u32[]{:S(2)}) copy-start(s32[1,32,96]{2,1,0:T(8,128)} %param.10) | copy-start | bytes 36868
  1.0 2.1 %copy-start.3 = (bf16[1,224,2048]{2,1,0:T(8,128)(2,1)S(1)}, bf16[1,224,2048]{2,1,0:T(8,128)(2,1)}, u32[]{:S(2)}) copy-start(bf16[1,224,2048]{2,1,0:T(8,128)(2,1)} %down_in.1) | copy-start | bytes 2752516
  1.7 1.5 %copy-start.1 = (bf16[1,2048,224]{1,2,0:T(8,128)(2,1)S(1)}, bf16[1,2048,224]{1,2,0:T(8,128)(2,1)}, u32[]{:S(2)}) copy-start(bf16[1,2048,224]{1,2,0:T(8,128)(2,1)} %param.11) | copy-start | bytes 2752516
  1.7 1.5 %copy-start.2 = (bf16[1,2048,224]{1,2,0:T(8,128)(2,1)S(1)}, bf16[1,2048,224]{1,2,0:T(8,128)(2,1)}, u32[]{:S(2)}) copy-start(bf16[1,2048,224]{1,2,0:T(8,128)(2,1)} %param.12) | copy-start | bytes 2752516

commit v4 on v1

--- a/solution.py
+++ b/solution.py
@@ -14,7 +14,8 @@
 
 def layer_kernel(
     n_dp,
-    packed,
+    packed_tokens,
+    packed_grads,
     collect,
     collect_t,
     gain,
@@ -78,6 +79,7 @@
     left = {"dp": lax.rem(dp + n_dp - 2, n_dp)}
     pair = {"expert": me + 1 - 2 * q}
     other = {"etp": 1 - etp}
+    packed = (packed_tokens, packed_grads)
     weights = ((gate_in, w_gate), (up_in, w_up), (down_in, w_down))
 
     def remote(src, dst, send_sem, recv_sem, where):
@@ -101,7 +103,7 @@
     for peer in (core, right, left, other):
         pl.semaphore_signal(barrier, inc=1, device_id=peer, device_id_type=MESH)
     own_got = [
-        pltpu.make_async_copy(packed.at[kind, me], got.at[kind, me], z_own.at[kind])
+        pltpu.make_async_copy(packed[kind].at[me], got.at[kind, me], z_own.at[kind])
         for kind in range(2)
     ]
     own_weights = [
@@ -124,7 +126,7 @@
     def dispatch(kind):
         def send(peer):
             remote(
-                packed.at[kind, peer],
+                packed[kind].at[peer],
                 got.at[kind, me],
                 z_send.at[kind],
                 z_recv.at[kind],
@@ -143,8 +145,6 @@
         remote(src.at[0], dst.at[1], w_send.at[i], w_recv.at[i], core)
         for i, (src, dst) in enumerate(weights)
     ]
-    for copy in given_weights:
-        copy.start()
     dispatch(1)
 
     def spread(kind, side):
@@ -255,15 +255,17 @@
         lax.fori_loop(0, 4, one, 0)
 
     compact(0)
+    for copy in given_weights:
+        copy.start()
     swaps[0].wait_recv()
     for copy in spreads[0, 1]:
         copy.start()
     pass_on(0, 0)
+    compact(1)
+    pass_on(0, 1)
     for copy in own_weights + given_weights:
         copy.wait()
     first_products(0, 1)
-    compact(1)
-    pass_on(0, 1)
     first_products(1, 2)
     swaps[1].wait_recv()
     for copy in spreads[1, 1]:
@@ -357,7 +359,7 @@
     own_back.wait()
     all_of(returned, b_sem.at[0])
     for kind in range(2):
-        all_of(packed.at[kind], z_send.at[kind])
+        all_of(packed[kind], z_send.at[kind])
     copies = swaps + direct + relays + sums + [pair_swap, half_swap]
     for key in spreads:
         copies += spreads[key] + forwards[key]
@@ -366,8 +368,8 @@
     all_of(arrived, b_sem.at[1])
 
 
-def layer(n_dp, packed, collect, gain, gate, up, down):
-    holders, most_slots, half = packed.shape[1:]
+def layer(n_dp, packed_tokens, packed_grads, collect, gain, gate, up, down):
+    holders, most_slots, half = packed_tokens.shape
     count = collect.shape[0]
     quarter = half // 2
     slice_width = gate.shape[1]
@@ -381,7 +383,7 @@
     return pl.pallas_call(
         functools.partial(layer_kernel, n_dp),
         out_shape=jax.ShapeDtypeStruct((holders, most_slots, quarter), bf16),
-        in_specs=[any_spec, vmem_spec, vmem_spec, vmem_spec, any_spec, any_spec, any_spec],
+        in_specs=[any_spec, any_spec, vmem_spec, vmem_spec, vmem_spec, any_spec, any_spec, any_spec],
         out_specs=any_spec,
         scratch_shapes=[
             pltpu.VMEM((2, holders, most_slots, half), bf16),
@@ -429,7 +431,7 @@
         compiler_params=pltpu.CompilerParams(
             collective_id=0, has_side_effects=True, vmem_limit_bytes=40 * 1024 * 1024
         ),
-    )(packed, collect, collect.T, gain, gate, up, down)
+    )(packed_tokens, packed_grads, collect, collect.T, gain, gate, up, down)
 
 
 def body(tokens, cotangent, scores, chosen, w_gate, w_up, w_down):
@@ -468,13 +470,19 @@
     ).astype(jnp.bfloat16)
     gain = lax.dynamic_index_in_dim(scores[0], expert_id, 0, keepdims=False)[:, None]
 
-    stacked = jnp.stack([tokens, cotangent]).reshape(2, local_rows, 2, model_width // 2)
-    packed = jnp.einsum(
-        "ejk,akqd->aeqjd", sender, stacked, preferred_element_type=jnp.float32
-    ).astype(jnp.bfloat16)
+    def pack(values):
+        sent = jnp.einsum(
+            "ejk,kqd->eqjd",
+            sender,
+            values.reshape(local_rows, 2, model_width // 2),
+            preferred_element_type=jnp.float32,
+        ).astype(jnp.bfloat16)
+        return sent.reshape(holders, most_slots, model_width // 2)
+
     arrived = layer(
         lax.axis_size("dp"),
-        packed.reshape(2, holders, most_slots, model_width // 2),
+        pack(tokens),
+        pack(cotangent),
         collect.reshape(capacity, holders * most_slots),
         gain,
         jnp.swapaxes(w_gate, 1, 2),

time: 110 us -> 112 us (1.018)
    unnamed x12 -> x14, local copies, waits for them, and re-layouts: 0.1 us -> 1.78 us
where the time goes in v4:
time: 112 us; the launch traced here: 111 us
  Pallas kernels  106 us (95%)
  local copies, waits for them, and re-layouts  2.8 us (2%)
  matrix products  1.52 us (1%)
  other arithmetic  1.26 us (1%)
    pallas_call x1, Pallas kernels, layer(): pl.pallas_call(functools.partial(layer_kernel, n_dp), out_shape=jax.Shape...  106 us

profile of v4, /device:TPU:6, one launch (start us, length us, event | category | flops | bytes accessed | tf_op | source)
XLA Modules:
  0.0 111.5 jit_solution(3638796845747475372)
XLA Ops:
  0.0 0.0 copy-start
  0.0 0.0 copy-start.4
  0.0 0.8 subtract_bitcast_fusion
  0.8 0.0 copy-done.4
  0.8 0.1 convert_reduce_fusion.1
  0.9 0.1 iota_subtract_fusion
  1.0 0.0 copy-start.5
  1.0 0.2 fusion.3
  1.2 0.0 copy-start.6
  1.2 0.1 copy.28
  1.3 0.6 copy-done.5
  1.9 0.0 copy-start.1
  1.9 0.0 copy-start.2
  1.9 0.2 fusion
  2.2 0.3 copy.30
  2.4 0.0 copy-done.6
  2.5 0.2 fusion.1
  2.7 0.3 copy.32
  3.0 0.2 convert_reduce_fusion
  3.3 0.1 copy.33.collect
  3.4 0.0 copy-done
  3.4 0.1 copy.34.gain
  3.5 0.0 copy-done.1
  3.5 0.0 copy-done.2
  3.5 0.0 copy-start.3
  3.6 1.2 %copy-done.3 = bf16[1,224,2048]{2,1,0:T(8,128)(2,1)S(1)} copy-done((bf16[1,224,2048]{2,1,0:T(8,128)(2,1)S(1)}, bf16[1,224,2048]{2,1,0:T(8,128)(2,1)}, u32[]{:S(2)}) %copy-start.3) | copy-done | bytes 917528
  4.7 105.7 %shard_map.73 = bf16[64,2,512]{2,1,0:T(2,128)(2,1)S(1)} custom-call(bf16[64,2,1024]{2,1,0:T(2,128)(2,1)S(1)} %bitcast.65, bf16[64,2,1024]{2,1,0:T(2,128)(2,1)S(1)} %bitcast.66, bf16[96,128]{1,0:T(8,128)(2,1)S(1)} %copy.33.collect, bf16[128,96]{1,0:T(8,128)(2,1)S(1)} %bitcast.71, f32[96,1]{1,0:T(8,128)S(1)} %copy.34.gain, bf16[1,224,2048]{2,1,0:T(8,128)(2,1)S(1)} %bitcast.67, ...), custom_call_target="tpu_custom_call" | custom-call | tf_op jit(solution)/shard_map/pallas_call | solution.py:383
  110.5 0.1 copy.35
  110.6 0.1 dot_general.20
  110.7 0.8 fusion.2
  (7 shorter events, 0.1 us)
Async XLA Ops:
  0.0 3.4 %copy-start = (f32[1,32,96]{2,1,0:T(8,128)S(1)}, f32[1,32,96]{2,1,0:T(8,128)}, u32[]{:S(2)}) copy-start(f32[1,32,96]{2,1,0:T(8,128)} %param.9) | copy-start | bytes 36868
  0.0 0.8 copy-start.4
  1.0 0.9 copy-start.5
  1.2 1.2 %copy-start.6 = (bf16[24,2048]{1,0:T(8,128)(2,1)S(1)}, bf16[24,2048]{1,0:T(8,128)(2,1)}, u32[]{:S(2)}) copy-start(bf16[24,2048]{1,0:T(8,128)(2,1)} %param.8) | copy-start | bytes 294916
  1.9 1.6 %copy-start.1 = (bf16[1,2048,224]{1,2,0:T(8,128)(2,1)S(1)}, bf16[1,2048,224]{1,2,0:T(8,128)(2,1)}, u32[]{:S(2)}) copy-start(bf16[1,2048,224]{1,2,0:T(8,128)(2,1)} %param.11) | copy-start | bytes 2752516
  1.9 1.6 %copy-start.2 = (bf16[1,2048,224]{1,2,0:T(8,128)(2,1)S(1)}, bf16[1,2048,224]{1,2,0:T(8,128)(2,1)}, u32[]{:S(2)}) copy-start(bf16[1,2048,224]{1,2,0:T(8,128)(2,1)} %param.12) | copy-start | bytes 2752516
  3.5 1.2 %copy-start.3 = (bf16[1,224,2048]{2,1,0:T(8,128)(2,1)S(1)}, bf16[1,224,2048]{2,1,0:T(8,128)(2,1)}, u32[]{:S(2)}) copy-start(bf16[1,224,2048]{2,1,0:T(8,128)(2,1)} %down_in.1) | copy-start | bytes 2752516
